TPU v7x, 256 devices: a whole 4x4x8 slice. The times are simulated.
256 devices in a mesh: grp: 8 (over z_lo, core), dev: 32 (over x, y, z_hi).
Axes of the slice: x: 4, y: 4, z: 8 (z_hi: 2, z_lo: 4; z = z_hi * 4 + z_lo), core: 2. Of those that a mesh axis runs over, the one named last changes fastest.
Arguments:
- query_raw: bfloat16 [16384, 1024], P(('grp', 'dev')), may hold values from -6 to 6
- key_raw: bfloat16 [16384, 128], P(('grp', 'dev')), may hold values from -6 to 6
- resp_values: bfloat16 [16384, 128], P(('grp', 'dev')), may hold values from -6 to 6
- attn_out: bfloat16 [16384, 1024], P(('grp', 'dev')), may hold values from -3 to 3
- out_grad: bfloat16 [16384, 1024], P(('grp', 'dev')), may hold values from -6 to 6
- prompt_keys: bfloat16 [65536, 128], P(('grp', 'dev')), may hold values from -2 to 2
- prompt_values: bfloat16 [65536, 128], P(('grp', 'dev')), may hold values from -6 to 6
- query_gain: float32 [128], replicated, may hold values from 0.5 to 1.5
- key_gain: float32 [128], replicated, may hold values from 1.5 to 4
- resp_lengths: int32 [8, 64], P('grp'), may hold values from 1 to 63, as said below
- resp_holder: int32 [8, 64], P('grp'), may hold values from 0 to 31, as said below
Outputs:
- query_raw_grad: bfloat16 [16384, 1024], P(('grp', 'dev'))
- key_raw_grad: bfloat16 [16384, 128], P(('grp', 'dev'))
- resp_value_grad: bfloat16 [16384, 128], P(('grp', 'dev'))
- prompt_key_grad: float32 [65536, 128], P(('grp', 'dev'))
- prompt_value_grad: float32 [65536, 128], P(('grp', 'dev'))
- query_gain_grad: float32 [128], replicated
- key_gain_grad: float32 [128], replicated
Inputs may be any that keep to these rules, and one draw needn't show every extreme that they name: `resp_holder`: every device of a group holds exactly 2 responses. `resp_lengths`: the responses held by one device have lengths summing to at most 64; in each group at least one device holds responses whose lengths sum to exactly 64; the others may hold fewer.
All inputs are finite; a program needn't handle non-finite values.
Results may differ from a plain program's by a relative error of at most 0.03.
Values may be sent and summed in bfloat16 or wider, within the bound.
A program may use at most 64 MiB of HBM per device.

v0:
```python
import math

import jax
import jax.numpy as jnp
from jax import lax
from jax.sharding import PartitionSpec as P

norm_eps = 1e-06


def layout_rows(lengths, holders, device_idx, slots):
    own_len = jnp.where(holders == device_idx, lengths, 0)
    seg_ends = jnp.cumsum(own_len, dtype=jnp.int32)
    row_ids = jnp.arange(slots, dtype=jnp.int32)
    segment = jnp.sum(
        (seg_ends[None, :] <= row_ids[:, None]).astype(jnp.int32), axis=1, dtype=jnp.int32
    )
    is_valid = row_ids < seg_ends[-1]
    allowed = (segment[:, None] == segment[None, :]) & (row_ids[None, :] <= row_ids[:, None])
    allowed = allowed & is_valid[:, None] & is_valid[None, :]
    return (is_valid, allowed)


def rms_forward(raw, gains):
    widened = raw.astype(jnp.float32)
    inverse = lax.rsqrt(jnp.mean(widened * widened, axis=-1, keepdims=True) + norm_eps)
    return (widened, inverse, widened * inverse * gains)


def rms_backward(widened, inverse, gains, upstream):
    scaled = upstream * gains
    raw_grad = inverse * scaled - widened * inverse**3 * jnp.mean(
        scaled * widened, axis=-1, keepdims=True
    )
    gain_grad = jnp.sum((upstream * widened * inverse).reshape(-1, widened.shape[-1]), axis=0)
    return (raw_grad, gain_grad)


def local_terms(query_raw, key_raw, attn_out, out_grad, query_gain, key_gain, allowed):
    slots, head_dim = key_raw.shape
    head_num = query_raw.shape[1] // head_dim
    query_wide, query_inverse, query_normed = rms_forward(
        query_raw.reshape(slots, head_num, head_dim), query_gain
    )
    key_wide, key_inverse, key_normed = rms_forward(key_raw, key_gain)
    queries = query_normed.astype(jnp.bfloat16).reshape(slots * head_num, head_dim)
    own_keys = key_normed.astype(jnp.bfloat16)
    grad_rows = out_grad.reshape(slots * head_num, head_dim)
    products = (out_grad.astype(jnp.float32) * attn_out.astype(jnp.float32)).reshape(
        slots * head_num, head_dim
    )
    out_dot = jnp.sum(products, axis=1)
    score_scale = head_dim ** (-0.5)
    self_scores = jnp.dot(queries, own_keys.T, preferred_element_type=jnp.float32) * score_scale
    self_exp = jnp.where(
        jnp.repeat(allowed, head_num, axis=0), jnp.exp(self_scores), jnp.zeros_like(self_scores)
    )
    return (
        query_wide,
        query_inverse,
        key_wide,
        key_inverse,
        queries,
        own_keys,
        grad_rows,
        out_dot,
        self_exp,
    )


def self_grads(
    self_exp, norm_total, out_dot, queries, own_keys, grad_rows, resp_values, score_scale
):
    attn_prob = self_exp / norm_total[:, None]
    prob_low = attn_prob.astype(jnp.bfloat16)
    prob_grad = jnp.dot(grad_rows, resp_values.T, preferred_element_type=jnp.float32)
    score_grad = (attn_prob * (prob_grad - out_dot[:, None])).astype(jnp.bfloat16)
    query_part = jnp.dot(score_grad, own_keys, preferred_element_type=jnp.float32)
    key_grad = jnp.dot(score_grad.T, queries, preferred_element_type=jnp.float32) * score_scale
    value_grad = jnp.dot(prob_low.T, grad_rows, preferred_element_type=jnp.float32)
    return (query_part, key_grad, value_grad)


def prompt_totals(queries, keys, score_scale, block_len):

    def advance(running, key_block):
        scores = jnp.dot(queries, key_block.T, preferred_element_type=jnp.float32) * score_scale
        return (running + jnp.sum(jnp.exp(scores), axis=1), None)

    start = jnp.zeros((queries.shape[0],), jnp.float32)
    running, unused = lax.scan(advance, start, keys.reshape(-1, block_len, keys.shape[1]))
    return running


def prompt_grads(
    queries, grad_rows, keys, values, norm_total, out_dot, row_live, score_scale, block_len
):
    head_dim = keys.shape[1]

    def advance(running, blocks):
        key_block, val_block = blocks
        scores = jnp.dot(queries, key_block.T, preferred_element_type=jnp.float32) * score_scale
        attn_prob = jnp.exp(scores) / norm_total[:, None] * row_live[:, None]
        prob_low = attn_prob.astype(jnp.bfloat16)
        prob_grad = jnp.dot(grad_rows, val_block.T, preferred_element_type=jnp.float32)
        score_grad = (attn_prob * (prob_grad - out_dot[:, None])).astype(jnp.bfloat16)
        running = running + jnp.dot(score_grad, key_block, preferred_element_type=jnp.float32)
        key_part = jnp.dot(score_grad.T, queries, preferred_element_type=jnp.float32) * score_scale
        value_part = jnp.dot(prob_low.T, grad_rows, preferred_element_type=jnp.float32)
        return (running, (key_part, value_part))

    start = jnp.zeros((queries.shape[0], head_dim), jnp.float32)
    blocks = (keys.reshape(-1, block_len, head_dim), values.reshape(-1, block_len, head_dim))
    running, (key_grad, value_grad) = lax.scan(advance, start, blocks)
    return (running, key_grad.reshape(-1, head_dim), value_grad.reshape(-1, head_dim))


def shards(
    query_raw,
    key_raw,
    resp_values,
    attn_out,
    out_grad,
    prompt_keys,
    prompt_values,
    query_gain,
    key_gain,
    resp_lengths,
    resp_holder,
):
    slots, head_dim = key_raw.shape
    head_num = query_raw.shape[1] // head_dim
    score_scale = head_dim ** (-0.5)
    device_idx = lax.axis_index("dev")
    lengths = resp_lengths[0]
    holders = resp_holder[0]
    is_valid, allowed = layout_rows(lengths, holders, device_idx, slots)
    terms = local_terms(query_raw, key_raw, attn_out, out_grad, query_gain, key_gain, allowed)
    (
        query_wide,
        query_inverse,
        key_wide,
        key_inverse,
        queries,
        own_keys,
        grad_rows,
        out_dot,
        self_exp,
    ) = terms
    self_sum = jnp.sum(self_exp, axis=1)
    whole_keys, whole_values = (
        lax.all_gather(prompt_keys, "dev", axis=0, tiled=True),
        lax.all_gather(prompt_values, "dev", axis=0, tiled=True),
    )
    block_len = math.gcd(whole_keys.shape[0], 2048)
    norm_total = prompt_totals(queries, whole_keys, score_scale, block_len) + self_sum
    row_live = jnp.repeat(is_valid, head_num).astype(jnp.float32)
    prompt_query, key_terms, value_terms = prompt_grads(
        queries,
        grad_rows,
        whole_keys,
        whole_values,
        norm_total,
        out_dot,
        row_live,
        score_scale,
        block_len,
    )
    key_grad, value_grad = (
        lax.psum_scatter(
            key_terms.astype(jnp.bfloat16), "dev", scatter_dimension=0, tiled=True
        ).astype(jnp.float32),
        lax.psum_scatter(
            value_terms.astype(jnp.bfloat16), "dev", scatter_dimension=0, tiled=True
        ).astype(jnp.float32),
    )
    self_query, self_key, self_value = self_grads(
        self_exp, norm_total, out_dot, queries, own_keys, grad_rows, resp_values, score_scale
    )
    query_norm_grad = (score_scale * (prompt_query + self_query)).reshape(slots, head_num, head_dim)
    query_raw_grad, query_gain_part = rms_backward(
        query_wide, query_inverse, query_gain, query_norm_grad
    )
    key_raw_grad, key_gain_part = rms_backward(key_wide, key_inverse, key_gain, self_key)
    query_gain_grad, key_gain_grad = lax.psum((query_gain_part, key_gain_part), ("grp", "dev"))
    return (
        query_raw_grad.reshape(slots, head_num * head_dim).astype(jnp.bfloat16),
        key_raw_grad.astype(jnp.bfloat16),
        self_value.astype(jnp.bfloat16),
        key_grad,
        value_grad,
        query_gain_grad,
        key_gain_grad,
    )


def solution(mesh):
    placed = (
        P(("grp", "dev"), None),
        P(("grp", "dev"), None),
        P(("grp", "dev"), None),
        P(("grp", "dev"), None),
        P(("grp", "dev"), None),
        P(("grp", "dev"), None),
        P(("grp", "dev"), None),
        P(),
        P(),
        P("grp", None),
        P("grp", None),
    )
    return jax.shard_map(
        shards,
        mesh=mesh,
        in_specs=placed,
        out_specs=(
            P(("grp", "dev"), None),
            P(("grp", "dev"), None),
            P(("grp", "dev"), None),
            P(("grp", "dev"), None),
            P(("grp", "dev"), None),
            P(),
            P(),
        ),
        check_vma=False,
    )
```

profile of v0, /device:TPU:32, one launch (start us, length us, event | category | flops | bytes accessed | tf_op | source)
XLA Modules:
  0.0 698.1 jit_solution(5573257155531115291)
XLA Ops:
  7.3 0.7 all-gather.3.cloned.1.call-update
  8.0 0.7 all-gather.5.cloned.1.call-update
  8.8 0.7 fusion.39
  9.6 0.1 reduce.2
  9.8 0.5 slice.5
  10.3 1.0 reshape.160
  11.2 0.9 multiply_bitcast_fusion
  12.2 0.1 reduce_sum.90
  12.5 0.7 iota_compare_fusion.2
  13.4 0.1 copy.22
  13.7 0.1 reduce_sum.94
  13.9 0.7 fusion.40
  14.7 0.1 multiply_convert_fusion.1
  14.8 0.2 fusion.41
  15.0 90.1 %all-gather.3.cloned.1.call-done = bf16[8192,128]{1,0:T(8,128)(2,1)} async-done(((bf16[256,128]{1,0:T(8,128)(2,1)}), bf16[8192,128]{1,0:T(8,128)(2,1)}) %all-gather.3.cloned.1.call-update) | async-done | bytes 2097168 | tf_op jit(solution)/shard_map/all_gather | solution.py:152
  105.1 7.2 %while.26 = (s32[]{:T(128)}, f32[512]{0:T(512)S(1)}, bf16[4,2048,128]{2,1,0:T(8,128)(2,1)}, bf16[512,128]{1,0:T(8,128)(2,1)S(1)}, s32[]{:T(128)}, /*index=5*/s32[]{:T(128)}) while((s32[]{:T(128)}, f32[512]{0:T(512)S(1)}, bf16[4,2048,128]{2,1,0:T(8,128)(2,1)}, bf16[512,128]{1,0:T(8,128)(2,1)S(1)}, s32[]{:T(128)}, ...), condition=%wide.region_3.4_spmd.clone, body=%wide.region_1.3_spmd.clone.sunk | while | flops 270533120 | bytes 663643 | solution.py:91
  105.1 1.8 exponential_reduce_fusion.2
  106.9 1.8 exponential_reduce_fusion.2
  108.7 1.8 exponential_reduce_fusion.2
  110.5 1.8 exponential_reduce_fusion.2
  112.3 81.9 %all-gather.5.cloned.1.call-done = bf16[8192,128]{1,0:T(8,128)(2,1)} async-done(((bf16[256,128]{1,0:T(8,128)(2,1)}), bf16[8192,128]{1,0:T(8,128)(2,1)}) %all-gather.5.cloned.1.call-update) | async-done | bytes 2097168 | tf_op jit(solution)/shard_map/all_gather | solution.py:153
  194.2 41.0 %while.27 = (s32[]{:T(128)}, f32[512,128]{1,0:T(8,128)S(1)}, bf16[4,2048,128]{2,1,0:T(8,128)(2,1)}, bf16[4,2048,128]{2,1,0:T(8,128)(2,1)}, bf16[4,2048,128]{2,1,...) while((s32[]{:T(128)}, f32[512,128]{1,0:T(8,128)S(1)}, ...), condition=%wide.region_10.11_spmd.clone, body=%wide.region_9.10_spmd.clone.sunk | while | flops 1349910528 | bytes 73937432 | solution.py:114
  194.4 1.9 divide_multiply_fusion.2
  196.4 2.2 multiply_convert_fusion.3
  198.6 2.0 convolution_add_fusion.3
  200.6 1.6 fusion.82
  202.1 0.1 copy-done.3
  202.2 0.9 fusion.83
  203.2 1.3 copy-done.4
  204.7 1.9 divide_multiply_fusion.2
  206.6 2.2 multiply_convert_fusion.3
  208.8 2.0 convolution_add_fusion.3
  210.8 1.6 fusion.82
  212.5 0.9 fusion.83
  213.5 1.3 copy-done.4
  214.9 1.9 divide_multiply_fusion.2
  216.9 2.2 multiply_convert_fusion.3
  219.1 2.0 convolution_add_fusion.3
  221.1 1.5 fusion.82
  222.6 0.2 copy-done.3
  222.7 0.9 fusion.83
  223.7 1.3 copy-done.4
  225.2 1.9 divide_multiply_fusion.2
  227.1 2.2 multiply_convert_fusion.3
  229.3 2.0 convolution_add_fusion.3
  231.3 1.5 fusion.82
  232.8 0.2 copy-done.3
  233.0 0.9 fusion.83
  233.9 1.3 copy-done.4
  235.3 0.5 reduce-scatter.5.cloned.1.call-update
  235.9 0.2 fusion.21
  236.1 0.4 multiply_reduce_fusion
  236.6 0.3 fusion.33
  236.9 76.5 %all-reduce = (f32[128]{0:T(128)}, f32[128]{0:T(128)}) all-reduce(f32[128]{0:T(128)S(1)} %get-tuple-element.146, f32[128]{0:T(128)S(1)} %get-tuple-element.148), channel_id=1, replica_groups=mesh['grp'=8,'dev'=32] {'grp','dev'}, use_global_device_ids=true, to_apply=%region_16.17 | all-reduce | flops 256 | bytes 2048 | tf_op jit(solution)/shard_map/psum | solution.py:185
  313.4 0.7 fusion.30
  314.1 0.8 convolution_convert_fusion
  314.9 0.1 mul.238
  315.0 0.1 mul.230
  315.1 0.1 mul.208
  315.3 0.8 fusion.23
  316.1 146.4 %reduce-scatter.3.cloned.1.call-done = bf16[256,128]{1,0:T(8,128)(2,1)} async-done(((bf16[8192,128]{1,0:T(8,128)(2,1)}), bf16[256,128]{1,0:T(8,128)(2,1)}) %reduce-scatter.3.cloned.1.call-update) | async-done | bytes 65552 | tf_op jit(solution)/shard_map/reduce_scatter | solution.py:170
  462.5 1.5 convert_element_type.96
  464.0 226.0 %reduce-scatter.5.cloned.1.call-done = bf16[256,128]{1,0:T(8,128)(2,1)} async-done(((bf16[8192,128]{1,0:T(8,128)(2,1)}), bf16[256,128]{1,0:T(8,128)(2,1)}) %reduce-scatter.5.cloned.1.call-update) | async-done | bytes 65552 | tf_op jit(solution)/shard_map/reduce_scatter | solution.py:173
  690.0 1.5 convert_element_type.99
  (81 shorter events, 2.0 us)
Async XLA Ops:
  7.2 228.7 %copy-start = (bf16[64,128]{1,0:T(8,128)(2,1)S(1)}, bf16[64,128]{1,0:T(8,128)(2,1)}, u32[]{:S(2)}) copy-start(bf16[64,128]{1,0:T(8,128)(2,1)} %param.17) | copy-start | bytes 49156
  7.2 6.3 copy-start.6
  7.2 6.4 copy-start.8
  7.2 7.3 %copy-start.7 = (bf16[64,128]{1,0:T(8,128)(2,1)S(1)}, bf16[64,128]{1,0:T(8,128)(2,1)}, u32[]{:S(2)}) copy-start(bf16[64,128]{1,0:T(8,128)(2,1)} %param.16) | copy-start | bytes 49156
  7.2 7.4 %copy-start.9 = (f32[128]{0:T(128)S(1)}, f32[128]{0:T(128)}, u32[]{:S(2)}) copy-start(f32[128]{0:T(128)} %param.22) | copy-start | bytes 1540
  7.2 7.6 %copy-start.10 = (f32[128]{0:T(128)S(1)}, f32[128]{0:T(128)}, u32[]{:S(2)}) copy-start(f32[128]{0:T(128)} %param.23) | copy-start | bytes 1540
  7.2 97.9 %all-gather.3.cloned.1.call-start = ((), (), s32[]{:S(2)}) async-start(), calls=%async_computation.2 | async-start | bytes 2162688 | tf_op jit(solution)/shard_map/all_gather | solution.py:152
  8.0 186.3 %all-gather.5.cloned.1.call-start = ((), (), s32[]{:S(2)}) async-start(), calls=%async_computation.3 | async-start | bytes 2162688 | tf_op jit(solution)/shard_map/all_gather | solution.py:153
  8.7 453.8 %reduce-scatter.3.cloned.1.call-start = ((), (), s32[]{:S(2)}) async-start(), calls=%async_computation.4 | async-start | bytes 2162688 | tf_op jit(solution)/shard_map/reduce_scatter | solution.py:170
  196.4 2.2 copy-start.1
  198.6 3.6 copy-start.2
  200.6 1.7 copy-start.3
  203.2 1.3 copy-start.4
  206.6 2.2 copy-start.1
  208.8 3.6 copy-start.2
  210.8 1.7 copy-start.3
  213.4 1.3 copy-start.4
  216.9 2.2 copy-start.1
  219.1 3.5 copy-start.2
  221.1 1.7 copy-start.3
  223.7 1.3 copy-start.4
  227.1 2.2 copy-start.1
  229.3 3.5 copy-start.2
  231.3 1.7 copy-start.3
  233.9 1.3 copy-start.4
  235.3 454.8 %reduce-scatter.5.cloned.1.call-start = ((), (), s32[]{:S(2)}) async-start(), calls=%async_computation.5 | async-start | bytes 2162688 | tf_op jit(solution)/shard_map/reduce_scatter | solution.py:173
  235.8 79.4 %copy-start.5 = (bf16[64,1024]{1,0:T(8,128)(2,1)S(1)}, bf16[64,1024]{1,0:T(8,128)(2,1)}, u32[]{:S(2)}) copy-start(bf16[64,1024]{1,0:T(8,128)(2,1)} %param.15) | copy-start | bytes 393220
Sparse Core Ops, SparseCore 0:
  11.5 93.5 all-gather.2
  108.5 85.6 all-gather.4
  235.4 227.0 reduce-scatter.2
  465.0 224.9 reduce-scatter.4
where the time goes:
time: 699 us; the launch traced here: 698 us
  waiting for transfers between devices  546 us (78%)
  blocking collectives  76.5 us (11%)
  matrix products  43.1 us (6%)
  between operations  14.1 us (2%)
  local copies, waits for them, and re-layouts  8.92 us (1%)
  other arithmetic  8.47 us (1%)
    reduce_scatter x1, waiting for transfers between devices, shards(): lax.psum_scatter(value_terms.astype(jnp.bfloat16), 'dev', scatter_dimensi...  226 us
    reduce_scatter x1, waiting for transfers between devices, shards(): lax.psum_scatter(key_terms.astype(jnp.bfloat16), 'dev', scatter_dimension...  146 us
    all_gather x1, waiting for transfers between devices, shards(): lax.all_gather(prompt_keys, 'dev', axis=0, tiled=True)  90.1 us
    all_gather x1, waiting for transfers between devices, shards(): lax.all_gather(prompt_values, 'dev', axis=0, tiled=True)  81.9 us
    psum x1, blocking collectives, shards(): lax.psum((query_gain_part, key_gain_part), ('grp', 'dev'))  76.5 us
    dot_general x8, matrix products, advance(): jnp.dot(queries, key_block.T, preferred_element_type=jnp.float32)  14.8 us
  transfers between devices with their start and end apart: 4, of which 4 were waited for; matrix products, arithmetic and copies ran while one was open for 3% of the time, Pallas kernels for 0%

commit v1 on v0

v1 whole, which is shorter than its diff:
```python
import functools
import math

import jax
import jax.numpy as jnp
from jax import lax
from jax.experimental import pallas as pl
from jax.experimental.pallas import tpu as pltpu
from jax.sharding import PartitionSpec as P

f32 = jnp.float32
bf16 = jnp.bfloat16
MESH = pl.DeviceIdType.MESH
EPS = 1e-06
HEADS = 8
HD = 128
CAP = 64
ROWS = HEADS * CAP
KEYS = 256
NT = (((1,), (1,)), ((), ()))
NN = (((1,), (0,)), ((), ()))
TN = (((0,), (0,)), ((), ()))
S_Q, S_D, S_K, S_N, S_G, S_R, S_Z, S_X, S_Y, S_V, S_C = 0, 4, 8, 16, 20, 24, 40, 42, 46, 50, 58
N_SEM = 60


def dot(a, b, dims):
    return lax.dot_general(a, b, dims, preferred_element_type=f32)


def kernel(
    qr_ref, kr_ref, rv_ref, ao_ref, og_ref, pk_ref, pv_ref, qg_ref, kg_ref, len_ref, hold_ref,
    oq_ref, ok_ref, ov_ref, opk_ref, opv_ref, oqg_ref, okg_ref,
    qb, db, kb, kt, eg, dqt, rs, rss, rsr, qn, invr, dqs, dqsend, dqr,
    se, sg, sb, acc, rr, zs, zr, gx, gy, gz, gc, gsrc, send, recv,
):
    grp = lax.axis_index("grp")
    dev = lax.axis_index("dev")
    x, y, z = dev // 8, (dev // 2) % 4, (dev % 2) * 4 + grp // 2
    core = grp % 2
    scale = HD ** (-0.5)

    def at(x=x, y=y, z=z, core=core):
        return ((z % 4) * 2 + core, x * 8 + y * 2 + z // 4)

    def xk(k):
        return at(x=(x + 4 - k) % 4)

    def yk(k):
        return at(y=(y + 4 - k) % 4)

    def zk(k):
        return at(z=(z + 8 - k) % 8)

    def copy(src, dst, sem, to):
        return pltpu.make_async_remote_copy(
            src_ref=src, dst_ref=dst, send_sem=send.at[sem], recv_sem=recv.at[sem],
            device_id=to, device_id_type=MESH,
        )

    def q_copy(k):
        return copy(qb.at[0], qb.at[k], S_Q + k, xk(k))

    def d_copy(k):
        return copy(db.at[0], db.at[k], S_D + k, xk(k))

    def k_copy(j):
        if j == 4:
            return copy(kb.at[0], kb.at[4], S_K + 4, zk(4))
        return copy(kb.at[j // 4 * 4], kb.at[j], S_K + j, yk(j % 4))

    def n_copy(k):
        return copy(rss, rsr.at[k], S_N + k, xk(k))

    def g_copy(k):
        return copy(dqsend.at[4 - k], dqr.at[k], S_G + k, xk(k))

    def r_copy(plane, t, kk):
        s = (4 - kk) % 4
        return copy(
            sb.at[plane, t, kk], rr.at[plane, t, s], S_R + plane * 8 + t * 4 + s, yk(s)
        )

    def z_copy(t):
        return copy(zs.at[t], zr.at[t], S_Z + t, zk(4))

    def gx_copy(k):
        return copy(gsrc.at[0], gx.at[x], S_X + k, xk(k))

    def gy_copy(k):
        return copy(gsrc.at[1], gy.at[y], S_Y + k, yk(k))

    def gz_copy(k):
        return copy(gsrc.at[2], gz.at[z], S_V + k, zk(k))

    def gc_copy():
        return copy(gsrc.at[3], gc.at[core], S_C, at(core=1 - core))

    barrier = pltpu.get_barrier_semaphore()
    partners = [xk(k) for k in (1, 2, 3)] + [yk(k) for k in (1, 2, 3)]
    partners += [zk(k) for k in range(1, 8)] + [at(core=1 - core)]
    for to in partners:
        pl.semaphore_signal(barrier, inc=1, device_id=to, device_id_type=MESH)

    kb[0, 0] = pk_ref[...]
    kb[0, 1] = pv_ref[...]
    held = hold_ref[...] == dev
    mine = jnp.where(held, len_ref[...].astype(f32), 0.0)
    place = lax.broadcasted_iota(jnp.int32, (1, 64), 1).astype(f32)
    total = jnp.sum(mine, axis=1, keepdims=True)
    first = jnp.min(jnp.where(held, place, 64.0), axis=1, keepdims=True)
    len1 = jnp.sum(jnp.where(place == first, mine, 0.0), axis=1, keepdims=True)
    live = lax.broadcasted_iota(jnp.int32, (CAP, HD), 0).astype(f32) < total
    gain = qg_ref[...]

    def q_head(h):
        wide = qr_ref[:, h * HD : (h + 1) * HD].astype(f32)
        inv = lax.rsqrt(jnp.mean(wide * wide, axis=1, keepdims=True) + EPS)
        return wide, inv

    ones = jnp.ones((8, HD), bf16)
    for h in range(HEADS):
        cols = slice(h * HD, (h + 1) * HD)
        rows = slice(h * CAP, (h + 1) * CAP)
        wide, inv = q_head(h)
        normed = wide * inv * (gain * (scale * math.log2(math.e)))
        qb[0, 0, rows, :] = jnp.where(live, normed, 0.0).astype(bf16)
        grad = jnp.where(live, og_ref[:, cols].astype(f32), 0.0)
        qb[0, 1, rows, :] = grad.astype(bf16)
        prod = grad * ao_ref[:, cols].astype(f32)
        high = prod.astype(bf16)
        low = (prod - high.astype(f32)).astype(bf16)
        sb[0, 0, h // 4, (h % 4) * CAP : (h % 4 + 1) * CAP, :] = high
        sb[0, 1, h // 4, (h % 4) * CAP : (h % 4 + 1) * CAP, :] = low
    for half in range(2):
        lanes = slice(half * KEYS, (half + 1) * KEYS)
        db[0, :, lanes] = dot(ones, sb[0, 0, half], NT) + dot(ones, sb[0, 1, half], NT)

    pl.semaphore_wait(barrier, len(partners))
    k_copy(4).start()
    for j in (2, 1, 3):
        k_copy(j).start()
    for k in (1, 3, 2):
        q_copy(k).start()
        d_copy(k).start()

    key_wide = kr_ref[...].astype(f32)
    key_inv = lax.rsqrt(jnp.mean(key_wide * key_wide, axis=1, keepdims=True) + EPS)
    own_keys = (key_wide * key_inv * kg_ref[...]).astype(bf16)
    slot_j = lax.broadcasted_iota(jnp.int32, (CAP, ROWS), 0)
    slot_i = lax.broadcasted_iota(jnp.int32, (CAP, ROWS), 1) & (CAP - 1)
    slot_j, slot_i = slot_j.astype(f32), slot_i.astype(f32)
    seg_j = jnp.where(slot_j >= len1, 1.0, 0.0)
    seg_i = jnp.where(slot_i >= len1, 1.0, 0.0)
    allowed = (slot_j <= slot_i) & (slot_i < total) & (seg_j == seg_i)
    e = jnp.where(allowed, jnp.exp2(dot(own_keys, qb[0, 0], NT)), 0.0)
    g = e * (dot(rv_ref[...], qb[0, 1], NT) - db[0, 0:1, :])
    rs[0] = jnp.sum(e.reshape(CAP // 8, 8, ROWS), axis=0)
    for i in range(1, 4):
        rs[i] = jnp.zeros((8, ROWS), f32)
    se[...] = e.astype(bf16)
    sg[...] = g.astype(bf16)
    dqs[...] = dot(own_keys, sg[...], TN)

    def block(keys, values, i):
        n = keys.shape[0]
        e = jnp.exp2(dot(keys, qb[i, 0], NT)).reshape(n // 8, 8, ROWS)
        rs[i] += jnp.sum(e, axis=0)
        p = dot(values, qb[i, 1], NT).reshape(n // 8, 8, ROWS)
        g = e * (p - db[i][None])
        return e.reshape(n, ROWS).astype(bf16), g.reshape(n, ROWS).astype(bf16)

    kt[:, 0:KEYS] = kb[0, 0].T
    for j in (1, 3, 2):
        k_copy(j).wait_recv()
        kt[:, j * KEYS : (j + 1) * KEYS] = kb[j, 0].T

    def near(m, carry):
        i = jnp.where(m == 2, 3, jnp.where(m == 3, 2, m))

        for k, step in ((1, 1), (3, 2), (2, 3)):

            @pl.when(m == step)
            def _():
                q_copy(k).wait_recv()
                d_copy(k).wait_recv()

        @pl.when(m == 2)
        def _():
            k_copy(4).wait_recv()
            for j in (6, 5, 7):
                k_copy(j).start()

        e, g = block(
            kb[0:4, 0].reshape(4 * KEYS, HD), kb[0:4, 1].reshape(4 * KEYS, HD), i
        )
        eg[0, 0:4, i] = e.reshape(4, KEYS, ROWS)
        eg[1, 0:4, i] = g.reshape(4, KEYS, ROWS)
        dqt[i] = dot(kt[...], g, NN)
        return carry

    lax.fori_loop(0, 4, near, 0)

    def far(m, carry):
        j = jnp.where(m == 2, 7, jnp.where(m == 3, 6, m + 4))

        for jj, step in ((5, 1), (7, 2), (6, 3)):

            @pl.when(m == step)
            def _():
                k_copy(jj).wait_recv()

        keys, values = kb[j, 0], kb[j, 1]
        turned = keys.T
        for i in range(4):
            e, g = block(keys, values, i)
            eg[0, j, i] = e
            eg[1, j, i] = g
            dqt[i] += dot(turned, g, NN)
        return carry

    lax.fori_loop(0, 4, far, 0)

    rss[...] = jnp.zeros((8, ROWS), f32)
    for i in range(4):
        rss[i : i + 1, :] = jnp.sum(rs[i], axis=0, keepdims=True)
    for k in (2, 1, 3):
        n_copy(k).start()
    for i in (2, 1, 3):
        dqsend[i] = dqt[i].astype(bf16)
        g_copy(4 - i).start()
    for k in (1, 3, 2):
        n_copy(k).wait_recv()
    for i in range(4):
        norm = rss[i : i + 1, :]
        for k in (1, 2, 3):
            r = (i + 4 - k) % 4
            norm = norm + rsr[k, r : r + 1, :]
        inv = 1.0 / norm
        if i == 0:
            invr[...] = jnp.broadcast_to(inv, (8, ROWS))
        for c in range(4):
            part = slice(c * HD, (c + 1) * HD)
            column = jnp.broadcast_to(inv[:, part], (HD, HD)).T
            qn[0, i, part, :] = (qb[i, 1, part, :].astype(f32) * column).astype(bf16)
            column = column * math.log(2.0)
            qn[1, i, part, :] = (qb[i, 0, part, :].astype(f32) * column).astype(bf16)

    def plane_sum(plane, t):
        for s in (1, 3, 2):
            r_copy(plane, t, 4 - s).wait_recv()
        total = acc[plane, t]
        for s in (1, 2, 3):
            total = total + rr[plane, t, s].astype(f32)
        return total

    def to_plane(t):
        zs[t] = plane_sum(1, t).astype(bf16)
        z_copy(t).start()

    def terms(n, carry):
        plane = 1 - n // 8
        t = (n // 4) % 2
        m = n % 4
        kk = jnp.where(m == 0, 2, jnp.where(m == 2, 3, jnp.where(m == 3, 0, 1)))

        @pl.when(n == 12)
        def _():
            to_plane(0)

        j = plane * 4 + kk
        part = dot(eg[t, j, 0], qn[t, 0], NN)
        for i in range(1, 4):
            part = part + dot(eg[t, j, i], qn[t, i], NN)
        sb[plane, t, kk] = part.astype(bf16)

        @pl.when(m < 3)
        def _():
            r_copy(plane, t, kk).start()

        @pl.when(m == 3)
        def _():
            acc[plane, t] = part

        return carry

    lax.fori_loop(0, 16, terms, 0)
    to_plane(1)

    ov_ref[...] = dot(se[...], qn[0, 0], NN).astype(bf16)
    kng = dot(sg[...], qn[1, 0], NN)
    w = kng * kg_ref[...]
    mean = jnp.mean(w * key_wide, axis=1, keepdims=True)
    ok_ref[...] = (key_inv * w - key_wide * (key_inv * key_inv * key_inv * mean)).astype(bf16)
    key_gain = jnp.sum(kng * key_wide * key_inv, axis=0, keepdims=True)

    for k in (1, 3, 2):
        g_copy(k).wait_recv()
    query_gain = jnp.zeros((1, HD), f32)
    for c in range(4):
        part = slice(c * HD, (c + 1) * HD)
        turned = dqt[0, :, part] + dqs[:, part]
        for k in (1, 2, 3):
            turned = turned + dqr[k, :, part].astype(f32)
        grad = (turned * (invr[0:1, part] * scale)).T
        for h in (2 * c, 2 * c + 1):
            qng = grad[(h % 2) * CAP : (h % 2 + 1) * CAP, :]
            wide, inv = q_head(h)
            u = qng * gain
            mean = jnp.mean(u * wide, axis=1, keepdims=True)
            oq_ref[:, h * HD : (h + 1) * HD] = (inv * u - wide * (inv * inv * inv * mean)).astype(bf16)
            query_gain = query_gain + jnp.sum(qng * wide * inv, axis=0, keepdims=True)

    both = jnp.concatenate([query_gain, key_gain, jnp.zeros((6, HD), f32)], axis=0)
    gsrc[0] = both
    gx[x] = both
    for k in (2, 1, 3):
        gx_copy(k).start()

    near_sum = [plane_sum(0, 0), plane_sum(0, 1)]

    for k in (1, 3, 2):
        gx_copy(k).wait_recv()
    both = gx[0] + gx[1] + gx[2] + gx[3]
    gsrc[1] = both
    gy[y] = both
    for k in (2, 1, 3):
        gy_copy(k).start()
    opv_ref[...] = near_sum[0]
    opk_ref[...] = near_sum[1]
    for k in (1, 3, 2):
        gy_copy(k).wait_recv()
    both = gy[0] + gy[1] + gy[2] + gy[3]
    gsrc[2] = both
    gz[z] = both
    for k in (4, 3, 5, 2, 6, 1, 7):
        gz_copy(k).start()
    z_copy(0).wait_recv()
    opv_ref[...] += zr[0].astype(f32)
    z_copy(1).wait_recv()
    opk_ref[...] += zr[1].astype(f32)
    for k in range(1, 8):
        gz_copy(k).wait_recv()
    both = gz[0]
    for k in range(1, 8):
        both = both + gz[k]
    gsrc[3] = both
    gc[core] = both
    gc_copy().start()
    gc_copy().wait_recv()
    both = gc[0] + gc[1]
    oqg_ref[...] = both[0:1, :]
    okg_ref[...] = both[1:2, :]

    for j in range(1, 8):
        k_copy(j).wait_send()
    for k in (1, 2, 3):
        for make in (q_copy, d_copy, n_copy, g_copy, gx_copy, gy_copy):
            make(k).wait_send()
        for plane in range(2):
            for t in range(2):
                r_copy(plane, t, k).wait_send()
    for t in range(2):
        z_copy(t).wait_send()
    for k in range(1, 8):
        gz_copy(k).wait_send()
    gc_copy().wait_send()


def shards(qr, kr, rv, ao, og, pk, pv, qg, kg, lengths, holders):
    vmem = pl.BlockSpec(memory_space=pltpu.VMEM)
    outs = pl.pallas_call(
        kernel,
        name="attention_backward",
        out_shape=(
            jax.ShapeDtypeStruct((CAP, HEADS * HD), bf16),
            jax.ShapeDtypeStruct((CAP, HD), bf16),
            jax.ShapeDtypeStruct((CAP, HD), bf16),
            jax.ShapeDtypeStruct((KEYS, HD), f32),
            jax.ShapeDtypeStruct((KEYS, HD), f32),
            jax.ShapeDtypeStruct((1, HD), f32),
            jax.ShapeDtypeStruct((1, HD), f32),
        ),
        in_specs=[vmem] * 11,
        out_specs=(vmem,) * 7,
        scratch_shapes=[
            pltpu.VMEM((4, 2, ROWS, HD), bf16),
            pltpu.VMEM((4, 8, ROWS), f32),
            pltpu.VMEM((8, 2, KEYS, HD), bf16),
            pltpu.VMEM((HD, 4 * KEYS), bf16),
            pltpu.VMEM((2, 8, 4, KEYS, ROWS), bf16),
            pltpu.VMEM((4, HD, ROWS), f32),
            pltpu.VMEM((4, 8, ROWS), f32),
            pltpu.VMEM((8, ROWS), f32),
            pltpu.VMEM((4, 8, ROWS), f32),
            pltpu.VMEM((2, 4, ROWS, HD), bf16),
            pltpu.VMEM((8, ROWS), f32),
            pltpu.VMEM((HD, ROWS), f32),
            pltpu.VMEM((4, HD, ROWS), bf16),
            pltpu.VMEM((4, HD, ROWS), bf16),
            pltpu.VMEM((CAP, ROWS), bf16),
            pltpu.VMEM((CAP, ROWS), bf16),
            pltpu.VMEM((2, 2, 4, KEYS, HD), bf16),
            pltpu.VMEM((2, 2, KEYS, HD), f32),
            pltpu.VMEM((2, 2, 4, KEYS, HD), bf16),
            pltpu.VMEM((2, KEYS, HD), bf16),
            pltpu.VMEM((2, KEYS, HD), bf16),
            pltpu.VMEM((4, 8, HD), f32),
            pltpu.VMEM((4, 8, HD), f32),
            pltpu.VMEM((8, 8, HD), f32),
            pltpu.VMEM((2, 8, HD), f32),
            pltpu.VMEM((4, 8, HD), f32),
            pltpu.SemaphoreType.DMA((N_SEM,)),
            pltpu.SemaphoreType.DMA((N_SEM,)),
        ],
        compiler_params=pltpu.CompilerParams(
            collective_id=0, has_side_effects=True, vmem_limit_bytes=52 << 20
        ),
    )(qr, kr, rv, ao, og, pk, pv, qg.reshape(1, HD), kg.reshape(1, HD), lengths, holders)
    return (*outs[:5], outs[5].reshape(HD), outs[6].reshape(HD))


def solution(mesh):
    rows = P(("grp", "dev"), None)
    return jax.shard_map(
        shards,
        mesh=mesh,
        in_specs=(rows,) * 7 + (P(), P(), P("grp", None), P("grp", None)),
        out_specs=(rows,) * 5 + (P(), P()),
        check_vma=False,
    )
```

time: 699 us -> 71 us (0.10)
  the two profiles are of different devices: /device:TPU:32 before, /device:TPU:1 now
where the time goes in v1:
time: 71 us; the launch traced here: 70.6 us
  Pallas kernels  59.2 us (83%)
  local copies, waits for them, and re-layouts  10.7 us (15%)
    pallas_call x1, Pallas kernels, shards(): pl.pallas_call(kernel, name='attention_backward', out_shape=(jax.ShapeDty...  59.2 us
    unnamed x29, local copies, waits for them, and re-layouts  10.7 us

profile of v1, /device:TPU:1, one launch (start us, length us, event | category | flops | bytes accessed | tf_op | source)
XLA Modules:
  0.0 70.6 jit_solution(17477095837944154412)
XLA Ops:
  0.6 0.0 copy-start.10
  0.6 0.0 copy-start.7
  0.7 0.0 copy-start.8
  0.7 0.0 copy-start.9
  0.7 0.6 copy-done.10
  1.3 0.0 copy-done.7
  1.3 0.0 copy-done.8
  1.3 0.0 copy-done.9
  1.3 0.0 copy-start
  1.3 0.9 %copy-done = bf16[64,1024]{1,0:T(8,128)(2,1)S(1)} copy-done((bf16[64,1024]{1,0:T(8,128)(2,1)S(1)}, bf16[64,1024]{1,0:T(8,128)(2,1)}, u32[]{:S(2)}) %copy-start) | copy-done | bytes 131096
  2.2 0.0 copy-start.1
  2.2 0.9 %copy-done.1 = bf16[64,1024]{1,0:T(8,128)(2,1)S(1)} copy-done((bf16[64,1024]{1,0:T(8,128)(2,1)S(1)}, bf16[64,1024]{1,0:T(8,128)(2,1)}, u32[]{:S(2)}) %copy-start.1) | copy-done | bytes 131096
  3.1 0.0 copy-start.2
  3.2 0.9 %copy-done.2 = bf16[64,1024]{1,0:T(8,128)(2,1)S(1)} copy-done((bf16[64,1024]{1,0:T(8,128)(2,1)S(1)}, bf16[64,1024]{1,0:T(8,128)(2,1)}, u32[]{:S(2)}) %copy-start.2) | copy-done | bytes 131096
  4.1 0.0 copy-start.3
  4.1 0.8 %copy-done.3 = bf16[256,128]{1,0:T(8,128)(2,1)S(1)} copy-done((bf16[256,128]{1,0:T(8,128)(2,1)S(1)}, bf16[256,128]{1,0:T(8,128)(2,1)}, u32[]{:S(2)}) %copy-start.3) | copy-done | bytes 65560
  4.9 0.0 copy-start.4
  4.9 0.8 %copy-done.4 = bf16[256,128]{1,0:T(8,128)(2,1)S(1)} copy-done((bf16[256,128]{1,0:T(8,128)(2,1)S(1)}, bf16[256,128]{1,0:T(8,128)(2,1)}, u32[]{:S(2)}) %copy-start.4) | copy-done | bytes 65560
  5.7 0.0 copy-start.5
  5.7 0.7 %copy-done.5 = bf16[64,128]{1,0:T(8,128)(2,1)S(1)} copy-done((bf16[64,128]{1,0:T(8,128)(2,1)S(1)}, bf16[64,128]{1,0:T(8,128)(2,1)}, u32[]{:S(2)}) %copy-start.5) | copy-done | bytes 16408
  6.5 0.0 copy-start.6
  6.5 0.7 %copy-done.6 = bf16[64,128]{1,0:T(8,128)(2,1)S(1)} copy-done((bf16[64,128]{1,0:T(8,128)(2,1)S(1)}, bf16[64,128]{1,0:T(8,128)(2,1)}, u32[]{:S(2)}) %copy-start.6) | copy-done | bytes 16408
  7.2 59.2 %attention_backward.1 = (bf16[64,1024]{1,0:T(8,128)(2,1)S(1)}, bf16[64,128]{1,0:T(8,128)(2,1)S(1)}, bf16[64,128]{1,0:T(8,128)(2,1)S(1)}, f32[256,128]{1,0:T(8,12...) custom-call(bf16[64,1024]{1,0:T(8,128)(2,1)S(1)} %copy-done, ...), custom_call_target="tpu_custom_call" | custom-call | tf_op jit(solution)/shard_map/attention_backward/pallas_call | solution.py:372
  66.4 0.7 copy.25
  67.1 0.6 copy.26
  67.7 0.6 copy.27
  68.3 0.7 copy.28
  68.9 0.7 copy.29
  69.6 0.5 copy.30
  70.1 0.5 copy.31
Async XLA Ops:
  0.6 0.7 copy-start.10
  0.6 0.7 copy-start.7
  0.7 0.7 copy-start.8
  0.7 0.7 copy-start.9
  1.3 0.9 %copy-start = (bf16[64,1024]{1,0:T(8,128)(2,1)S(1)}, bf16[64,1024]{1,0:T(8,128)(2,1)}, u32[]{:S(2)}) copy-start(bf16[64,1024]{1,0:T(8,128)(2,1)} %qr_ref.1) | copy-start | bytes 393220
  2.2 0.9 %copy-start.1 = (bf16[64,1024]{1,0:T(8,128)(2,1)S(1)}, bf16[64,1024]{1,0:T(8,128)(2,1)}, u32[]{:S(2)}) copy-start(bf16[64,1024]{1,0:T(8,128)(2,1)} %ao_ref.1) | copy-start | bytes 393220
  3.1 0.9 %copy-start.2 = (bf16[64,1024]{1,0:T(8,128)(2,1)S(1)}, bf16[64,1024]{1,0:T(8,128)(2,1)}, u32[]{:S(2)}) copy-start(bf16[64,1024]{1,0:T(8,128)(2,1)} %og_ref.1) | copy-start | bytes 393220
  4.1 0.8 %copy-start.3 = (bf16[256,128]{1,0:T(8,128)(2,1)S(1)}, bf16[256,128]{1,0:T(8,128)(2,1)}, u32[]{:S(2)}) copy-start(bf16[256,128]{1,0:T(8,128)(2,1)} %pk_ref.1) | copy-start | bytes 196612
  4.9 0.8 %copy-start.4 = (bf16[256,128]{1,0:T(8,128)(2,1)S(1)}, bf16[256,128]{1,0:T(8,128)(2,1)}, u32[]{:S(2)}) copy-start(bf16[256,128]{1,0:T(8,128)(2,1)} %pv_ref.1) | copy-start | bytes 196612
  5.7 0.7 %copy-start.5 = (bf16[64,128]{1,0:T(8,128)(2,1)S(1)}, bf16[64,128]{1,0:T(8,128)(2,1)}, u32[]{:S(2)}) copy-start(bf16[64,128]{1,0:T(8,128)(2,1)} %kr_ref.1) | copy-start | bytes 49156
  6.5 0.7 %copy-start.6 = (bf16[64,128]{1,0:T(8,128)(2,1)S(1)}, bf16[64,128]{1,0:T(8,128)(2,1)}, u32[]{:S(2)}) copy-start(bf16[64,128]{1,0:T(8,128)(2,1)} %rv_ref.1) | copy-start | bytes 49156

commit v2 on v1

v2 whole, which is shorter than its diff:
```python
import functools
import math

import jax
import jax.numpy as jnp
from jax import lax
from jax.experimental import pallas as pl
from jax.experimental.pallas import tpu as pltpu
from jax.sharding import PartitionSpec as P

f32 = jnp.float32
bf16 = jnp.bfloat16
MESH = pl.DeviceIdType.MESH
EPS = 1e-06
HEADS = 8
HD = 128
CAP = 64
ROWS = HEADS * CAP
KEYS = 256
NT = (((1,), (1,)), ((), ()))
NN = (((1,), (0,)), ((), ()))
TN = (((0,), (0,)), ((), ()))
S_Q, S_D, S_K, S_N, S_G, S_R, S_Z, S_X, S_Y, S_V, S_C = 0, 8, 12, 28, 32, 36, 52, 54, 58, 62, 70
N_SEM = 71


def dot(a, b, dims):
    return lax.dot_general(a, b, dims, preferred_element_type=f32)


def kernel(
    qr_in, kr_in, rv_in, ao_in, og_in, pk_in, pv_in, qg_in, kg_in, len_in, hold_in,
    oq_out, ok_out, ov_out, opk_out, opv_out, oqg_out, okg_out,
    oq_ref, ok_ref, ov_ref, opk_ref, opv_ref, oqg_ref, okg_ref,
    qr_ref, kr_ref, rv_ref, ao_ref, og_ref, qg_ref, kg_ref, len_ref, hold_ref,
    qb, db, kb, kt, eg, dqt, rs, rss, rsr, qn, invr, dqs, dqsend, dqr,
    se, sg, sb, acc, rr, zs, zr, gx, gy, gz, gc, gsrc, send, recv, load, store,
):
    grp = lax.axis_index("grp")
    dev = lax.axis_index("dev")
    x, y, z = dev // 8, (dev // 2) % 4, (dev % 2) * 4 + grp // 2
    core = grp % 2
    scale = HD ** (-0.5)

    def at(x=x, y=y, z=z, core=core):
        return ((z % 4) * 2 + core, x * 8 + y * 2 + z // 4)

    def xk(k):
        return at(x=(x + 4 - k) % 4)

    def yk(k):
        return at(y=(y + 4 - k) % 4)

    def zk(k):
        return at(z=(z + 8 - k) % 8)

    def copy(src, dst, sem, to):
        return pltpu.make_async_remote_copy(
            src_ref=src, dst_ref=dst, send_sem=send.at[sem], recv_sem=recv.at[sem],
            device_id=to, device_id_type=MESH,
        )

    def q_copy(k, p):
        src = qb.at[0, p] if k != 2 else qb.at[3 - 2 * p, p]
        return copy(src, qb.at[k, p], S_Q + 2 * k + p, xk(k if k != 2 else 3 - 2 * p))

    def d_copy(k):
        return copy(db.at[0], db.at[k], S_D + k, xk(k))

    def k_copy(j, p):
        src = (pk_in, pv_in)[p] if j <= 4 else kb.at[4, p]
        return copy(src, kb.at[j, p], S_K + 2 * j + p, zk(4) if j == 4 else yk(j % 4))

    def n_copy(k):
        return copy(rss, rsr.at[k], S_N + k, xk(k))

    def g_copy(k):
        return copy(dqsend.at[4 - k], dqr.at[k], S_G + k, xk(k))

    def r_copy(plane, t, kk):
        s = (4 - kk) % 4
        return copy(
            sb.at[plane, t, kk], rr.at[plane, t, s], S_R + plane * 8 + t * 4 + s, yk(s)
        )

    def z_copy(t):
        return copy(zs.at[t], zr.at[t], S_Z + t, zk(4))

    def gx_copy(k):
        return copy(gsrc.at[0], gx.at[x], S_X + k, xk(k))

    def gy_copy(k):
        return copy(gsrc.at[1], gy.at[y], S_Y + k, yk(k))

    def gz_copy(k):
        return copy(gsrc.at[2], gz.at[z], S_V + k, zk(k))

    def gc_copy():
        return copy(gsrc.at[3], gc.at[core], S_C, at(core=1 - core))

    loads = [
        pltpu.make_async_copy(src, dst, load.at[n])
        for n, (src, dst) in enumerate(
            (
                (pk_in, kb.at[0, 0]), (pv_in, kb.at[0, 1]), (hold_in, hold_ref), (len_in, len_ref),
                (qg_in, qg_ref), (kg_in, kg_ref), (qr_in, qr_ref), (og_in, og_ref), (ao_in, ao_ref),
                (kr_in, kr_ref), (rv_in, rv_ref),
            )
        )
    ]
    for one in loads:
        one.start()

    stores = [
        pltpu.make_async_copy(src, dst, store.at[n])
        for n, (src, dst) in enumerate(
            (
                (oq_ref, oq_out), (ok_ref, ok_out), (ov_ref, ov_out), (opk_ref, opk_out),
                (opv_ref, opv_out), (oqg_ref, oqg_out), (okg_ref, okg_out),
            )
        )
    ]

    barrier = pltpu.get_barrier_semaphore()
    partners = [xk(k) for k in (1, 2, 3)] + [yk(k) for k in (1, 2, 3)]
    partners += [zk(k) for k in range(1, 8)] + [at(core=1 - core)]
    for to in partners:
        pl.semaphore_signal(barrier, inc=1, device_id=to, device_id_type=MESH)

    pl.semaphore_wait(barrier, len(partners))
    for p in range(2):
        k_copy(4, p).start()
    for p in range(2):
        for j in (1, 3, 2):
            k_copy(j, p).start()
    for one in loads:
        one.wait()
    held = hold_ref[...] == dev
    mine = jnp.where(held, len_ref[...].astype(f32), 0.0)
    place = lax.broadcasted_iota(jnp.int32, (1, 64), 1).astype(f32)
    total = jnp.sum(mine, axis=1, keepdims=True)
    first = jnp.min(jnp.where(held, place, 64.0), axis=1, keepdims=True)
    len1 = jnp.sum(jnp.where(place == first, mine, 0.0), axis=1, keepdims=True)
    live = lax.broadcasted_iota(jnp.int32, (CAP, HD), 0).astype(f32) < total
    gain = qg_ref[...]

    def q_head(h):
        wide = qr_ref[:, h * HD : (h + 1) * HD].astype(f32)
        inv = lax.rsqrt(jnp.mean(wide * wide, axis=1, keepdims=True) + EPS)
        return wide, inv

    ones = jnp.ones((8, HD), bf16)
    for h in range(HEADS):
        cols = slice(h * HD, (h + 1) * HD)
        rows = slice(h * CAP, (h + 1) * CAP)
        wide, inv = q_head(h)
        normed = wide * inv * (gain * (scale * math.log2(math.e)))
        qb[0, 0, rows, :] = jnp.where(live, normed, 0.0).astype(bf16)
        grad = jnp.where(live, og_ref[:, cols].astype(f32), 0.0)
        qb[0, 1, rows, :] = grad.astype(bf16)
        prod = grad * ao_ref[:, cols].astype(f32)
        high = prod.astype(bf16)
        low = (prod - high.astype(f32)).astype(bf16)
        sb[0, 0, h // 4, (h % 4) * CAP : (h % 4 + 1) * CAP, :] = high
        sb[0, 1, h // 4, (h % 4) * CAP : (h % 4 + 1) * CAP, :] = low
    for half in range(2):
        lanes = slice(half * KEYS, (half + 1) * KEYS)
        both = dot(ones, sb[0, 0, half], NT) + dot(ones, sb[0, 1, half], NT)
        db[0, :, lanes] = both[0:1, :]

    for p in range(2):
        q_copy(3, p).start()
        q_copy(1, 1 - p).start()
    for k in (1, 3, 2):
        d_copy(k).start()

    key_wide = kr_ref[...].astype(f32)
    key_inv = lax.rsqrt(jnp.mean(key_wide * key_wide, axis=1, keepdims=True) + EPS)
    own_keys = (key_wide * key_inv * kg_ref[...]).astype(bf16)
    slot_j = lax.broadcasted_iota(jnp.int32, (CAP, ROWS), 0)
    slot_i = lax.broadcasted_iota(jnp.int32, (CAP, ROWS), 1) & (CAP - 1)
    slot_j, slot_i = slot_j.astype(f32), slot_i.astype(f32)
    seg_j = jnp.where(slot_j >= len1, 1.0, 0.0)
    seg_i = jnp.where(slot_i >= len1, 1.0, 0.0)
    allowed = (slot_j <= slot_i) & (slot_i < total) & (seg_j == seg_i)
    e = jnp.where(allowed, jnp.exp2(dot(own_keys, qb[0, 0], NT)), 0.0)
    g = e * (dot(rv_ref[...], qb[0, 1], NT) - db[0])
    rs[0] = jnp.sum(e.reshape(CAP // 8, 8, ROWS), axis=0)
    for i in range(1, 4):
        rs[i] = jnp.zeros((8, ROWS), f32)
    se[...] = e.astype(bf16)
    sg[...] = g.astype(bf16)
    dqs[...] = dot(own_keys, sg[...], TN)

    def block(keys, values, i):
        n = keys.shape[0]
        e = jnp.exp2(dot(keys, qb[i, 0], NT))
        rs[i] += jnp.sum(e.reshape(n // 8, 8, ROWS), axis=0)
        g = e * (dot(values, qb[i, 1], NT) - db[i])
        return e.astype(bf16), g.astype(bf16)

    q_copy(3, 0).wait_recv()
    q_copy(2, 0).start()
    q_copy(1, 1).wait_recv()
    q_copy(2, 1).start()
    kt[0, :, 0:KEYS] = kb[0, 0].T
    for j in (1, 3, 2):
        k_copy(j, 0).wait_recv()
        kt[0, :, j * KEYS : (j + 1) * KEYS] = kb[j, 0].T
    for j in (1, 3, 2):
        k_copy(j, 1).wait_recv()

    def pass_on(p):
        k_copy(4, p).wait_recv()
        for j in (5, 7, 6):
            k_copy(j, p).start()

    pass_on(0)

    def near(m, carry):
        i = jnp.where(m == 2, 3, jnp.where(m == 3, 2, m))

        @pl.when(m == 1)
        def _():
            pass_on(1)
            q_copy(1, 0).wait_recv()
            d_copy(1).wait_recv()

        @pl.when(m == 2)
        def _():
            q_copy(3, 1).wait_recv()
            d_copy(3).wait_recv()

        @pl.when(m == 3)
        def _():
            q_copy(2, 0).wait_recv()
            q_copy(2, 1).wait_recv()
            d_copy(2).wait_recv()

        e, g = block(
            kb[0:4, 0].reshape(4 * KEYS, HD), kb[0:4, 1].reshape(4 * KEYS, HD), i
        )
        eg[0, 0:4, i] = e.reshape(4, KEYS, ROWS)
        eg[1, 0:4, i] = g.reshape(4, KEYS, ROWS)
        dqt[i] = dot(kt[0], g, NN)
        return carry

    lax.fori_loop(0, 4, near, 0)

    def far(m, carry):
        j = jnp.where(m == 2, 7, jnp.where(m == 3, 6, m + 4))

        for jj, step in ((5, 1), (7, 2), (6, 3)):

            @pl.when(m == step)
            def _():
                k_copy(jj, 0).wait_recv()
                k_copy(jj, 1).wait_recv()

        keys, values = kb[j, 0], kb[j, 1]
        for i in range(4):
            e, g = block(keys, values, i)
            eg[0, j, i] = e
            eg[1, j, i] = g
        return carry

    lax.fori_loop(0, 4, far, 0)

    for i in range(4):
        rss[i] = jnp.sum(rs[i], axis=0, keepdims=True)
    for k in (2, 1, 3):
        n_copy(k).start()

    for j in range(4):
        kt[1, :, j * KEYS : (j + 1) * KEYS] = kb[4 + j, 0].T

    def rest(m, carry):
        i = (m + 2) % 4
        dqt[i] += dot(kt[1], eg[1, 4:8, i].reshape(4 * KEYS, ROWS), NN)
        dqsend[i] = dqt[i].astype(bf16)

        for k in (1, 2, 3):

            @pl.when(i == 4 - k)
            def _():
                g_copy(k).start()

        return carry

    lax.fori_loop(0, 4, rest, 0)
    dqt[0] += dqs[...]
    dqsend[0] = dqt[0].astype(bf16)
    for k in (1, 3, 2):
        n_copy(k).wait_recv()
    for i in range(4):
        norm = rss[i]
        for k in (1, 2, 3):
            norm = norm + rsr[k, (i + 4 - k) % 4]
        inv = 1.0 / norm
        if i == 0:
            invr[...] = inv
        for c in range(4):
            part = slice(c * HD, (c + 1) * HD)
            column = jnp.broadcast_to(inv[:, part], (HD, HD)).T
            qn[0, i, part, :] = (qb[i, 1, part, :].astype(f32) * column).astype(bf16)
            column = column * math.log(2.0)
            qn[1, i, part, :] = (qb[i, 0, part, :].astype(f32) * column).astype(bf16)

    def plane_sum(plane, t):
        for s in (1, 3, 2):
            r_copy(plane, t, 4 - s).wait_recv()
        total = acc[plane, t]
        for s in (1, 2, 3):
            total = total + rr[plane, t, s].astype(f32)
        return total

    def to_plane(t):
        zs[t] = plane_sum(1, t).astype(bf16)
        z_copy(t).start()

    def own_terms():
        ov_ref[...] = dot(se[...], qn[0, 0], NN).astype(bf16)
        kng = dot(sg[...], qn[1, 0], NN)
        wide = kr_ref[...].astype(f32)
        inv = lax.rsqrt(jnp.mean(wide * wide, axis=1, keepdims=True) + EPS)
        w = kng * kg_ref[...]
        mean = jnp.mean(w * wide, axis=1, keepdims=True)
        ok_ref[...] = (inv * w - wide * (inv * inv * inv * mean)).astype(bf16)
        stores[1].start()
        stores[2].start()
        key_gain = jnp.sum(kng * wide * inv, axis=0, keepdims=True)
        square = dot(dqsend[0], qn[1, 0], NN)
        for i in range(1, 4):
            square = square + dot(dqsend[i], qn[1, i], NN)
        one = lax.broadcasted_iota(jnp.int32, (HD, HD), 0)
        two = lax.broadcasted_iota(jnp.int32, (HD, HD), 1)
        query_gain = jnp.sum(jnp.where(one == two, square, 0.0), axis=0, keepdims=True) / gain
        both = jnp.concatenate([query_gain, key_gain, jnp.zeros((6, HD), f32)], axis=0)
        gsrc[0] = both
        gx[x] = both
        for k in (2, 1, 3):
            gx_copy(k).start()

    def gains_y():
        for k in (1, 3, 2):
            gx_copy(k).wait_recv()
        both = gx[0] + gx[1] + gx[2] + gx[3]
        gsrc[1] = both
        gy[y] = both
        for k in (2, 1, 3):
            gy_copy(k).start()

    def gains_z():
        for k in (1, 3, 2):
            gy_copy(k).wait_recv()
        both = gy[0] + gy[1] + gy[2] + gy[3]
        gsrc[2] = both
        gz[z] = both
        for k in (4, 3, 5, 2, 6, 1, 7):
            gz_copy(k).start()

    def gains_core():
        for k in range(1, 8):
            gz_copy(k).wait_recv()
        both = gz[0]
        for k in range(1, 8):
            both = both + gz[k]
        gsrc[3] = both
        gc[core] = both
        gc_copy().start()

    def terms(n, carry):
        plane = 1 - n // 8
        t = (n // 4) % 2
        m = n % 4
        kk = jnp.where(m == 0, 2, jnp.where(m == 2, 3, jnp.where(m == 3, 0, 1)))

        @pl.when(n == 4)
        def _():
            own_terms()

        @pl.when(n == 8)
        def _():
            gains_y()

        @pl.when(n == 12)
        def _():
            to_plane(0)

        @pl.when(n == 13)
        def _():
            gains_z()

        j = plane * 4 + kk
        part = dot(eg[t, j, 0], qn[t, 0], NN)
        for i in range(1, 4):
            part = part + dot(eg[t, j, i], qn[t, i], NN)
        sb[plane, t, kk] = part.astype(bf16)

        @pl.when(m < 3)
        def _():
            r_copy(plane, t, kk).start()

        @pl.when(m == 3)
        def _():
            acc[plane, t] = part

        return carry

    lax.fori_loop(0, 16, terms, 0)
    to_plane(1)

    for k in (1, 3, 2):
        g_copy(k).wait_recv()
    for c in range(4):
        part = slice(c * HD, (c + 1) * HD)
        turned = dqt[0, :, part]
        for k in (1, 2, 3):
            turned = turned + dqr[k, :, part].astype(f32)
        grad = (turned * (invr[:, part] * scale)).T
        for h in (2 * c, 2 * c + 1):
            wide, inv = q_head(h)
            u = grad[(h % 2) * CAP : (h % 2 + 1) * CAP, :] * gain
            mean = jnp.mean(u * wide, axis=1, keepdims=True)
            found = inv * u - wide * (inv * inv * inv * mean)
            oq_ref[:, h * HD : (h + 1) * HD] = found.astype(bf16)
    stores[0].start()

    opv_ref[...] = plane_sum(0, 0)
    opk_ref[...] = plane_sum(0, 1)
    gains_core()
    z_copy(0).wait_recv()
    opv_ref[...] += zr[0].astype(f32)
    stores[4].start()
    z_copy(1).wait_recv()
    opk_ref[...] += zr[1].astype(f32)
    stores[3].start()
    gc_copy().wait_recv()
    both = gc[0] + gc[1]
    oqg_ref[...] = both[0:1, :]
    okg_ref[...] = both[1:2, :]
    stores[5].start()
    stores[6].start()

    for p in range(2):
        for j in range(1, 8):
            k_copy(j, p).wait_send()
        for k in (1, 2, 3):
            q_copy(k, p).wait_send()
    for k in (1, 2, 3):
        for make in (d_copy, n_copy, g_copy, gx_copy, gy_copy):
            make(k).wait_send()
        for plane in range(2):
            for t in range(2):
                r_copy(plane, t, k).wait_send()
    for t in range(2):
        z_copy(t).wait_send()
    for k in range(1, 8):
        gz_copy(k).wait_send()
    gc_copy().wait_send()
    for one in stores:
        one.wait()


def deliver(*refs):
    into, out = refs[21], refs[22]
    first = [pltpu.make_async_copy(refs[i], refs[14 + i], into.at[i]) for i in range(7)]
    then = [pltpu.make_async_copy(refs[14 + i], refs[7 + i], out.at[i]) for i in range(7)]
    for one in first:
        one.start()
    for one, two in zip(first, then, strict=True):
        one.wait()
        two.start()
    for two in then:
        two.wait()


def shards(qr, kr, rv, ao, og, pk, pv, qg, kg, lengths, holders):
    shapes = (
        jax.ShapeDtypeStruct((CAP, HEADS * HD), bf16),
        jax.ShapeDtypeStruct((CAP, HD), bf16),
        jax.ShapeDtypeStruct((CAP, HD), bf16),
        jax.ShapeDtypeStruct((KEYS, HD), f32),
        jax.ShapeDtypeStruct((KEYS, HD), f32),
        jax.ShapeDtypeStruct((1, HD), f32),
        jax.ShapeDtypeStruct((1, HD), f32),
    )
    somewhere = pl.BlockSpec(memory_space=pl.ANY)
    outs = pl.pallas_call(
        kernel,
        name="attention_backward",
        out_shape=shapes,
        in_specs=[somewhere] * 11,
        out_specs=(somewhere,) * 7,
        scratch_shapes=[
            pltpu.VMEM((CAP, HEADS * HD), bf16),
            pltpu.VMEM((CAP, HD), bf16),
            pltpu.VMEM((CAP, HD), bf16),
            pltpu.VMEM((KEYS, HD), f32),
            pltpu.VMEM((KEYS, HD), f32),
            pltpu.VMEM((1, HD), f32),
            pltpu.VMEM((1, HD), f32),
            pltpu.VMEM((CAP, HEADS * HD), bf16),
            pltpu.VMEM((CAP, HD), bf16),
            pltpu.VMEM((CAP, HD), bf16),
            pltpu.VMEM((CAP, HEADS * HD), bf16),
            pltpu.VMEM((CAP, HEADS * HD), bf16),
            pltpu.VMEM((1, HD), f32),
            pltpu.VMEM((1, HD), f32),
            pltpu.VMEM((1, 64), jnp.int32),
            pltpu.VMEM((1, 64), jnp.int32),
            pltpu.VMEM((4, 2, ROWS, HD), bf16),
            pltpu.VMEM((4, 1, ROWS), f32),
            pltpu.VMEM((8, 2, KEYS, HD), bf16),
            pltpu.VMEM((2, HD, 4 * KEYS), bf16),
            pltpu.VMEM((2, 8, 4, KEYS, ROWS), bf16),
            pltpu.VMEM((4, HD, ROWS), f32),
            pltpu.VMEM((4, 8, ROWS), f32),
            pltpu.VMEM((4, 1, ROWS), f32),
            pltpu.VMEM((4, 4, 1, ROWS), f32),
            pltpu.VMEM((2, 4, ROWS, HD), bf16),
            pltpu.VMEM((1, ROWS), f32),
            pltpu.VMEM((HD, ROWS), f32),
            pltpu.VMEM((4, HD, ROWS), bf16),
            pltpu.VMEM((4, HD, ROWS), bf16),
            pltpu.VMEM((CAP, ROWS), bf16),
            pltpu.VMEM((CAP, ROWS), bf16),
            pltpu.VMEM((2, 2, 4, KEYS, HD), bf16),
            pltpu.VMEM((2, 2, KEYS, HD), f32),
            pltpu.VMEM((2, 2, 4, KEYS, HD), bf16),
            pltpu.VMEM((2, KEYS, HD), bf16),
            pltpu.VMEM((2, KEYS, HD), bf16),
            pltpu.VMEM((4, 8, HD), f32),
            pltpu.VMEM((4, 8, HD), f32),
            pltpu.VMEM((8, 8, HD), f32),
            pltpu.VMEM((2, 8, HD), f32),
            pltpu.VMEM((4, 8, HD), f32),
            pltpu.SemaphoreType.DMA((N_SEM,)),
            pltpu.SemaphoreType.DMA((N_SEM,)),
            pltpu.SemaphoreType.DMA((11,)),
            pltpu.SemaphoreType.DMA((7,)),
        ],
        compiler_params=pltpu.CompilerParams(
            collective_id=0, has_side_effects=True, vmem_limit_bytes=60 << 20
        ),
    )(qr, kr, rv, ao, og, pk, pv, qg.reshape(1, HD), kg.reshape(1, HD), lengths, holders)
    outs = pl.pallas_call(
        deliver,
        name="deliver",
        out_shape=shapes,
        in_specs=[somewhere] * 7,
        out_specs=(somewhere,) * 7,
        scratch_shapes=[pltpu.VMEM(shape.shape, shape.dtype) for shape in shapes]
        + [pltpu.SemaphoreType.DMA((7,))] * 2,
        compiler_params=pltpu.CompilerParams(vmem_limit_bytes=60 << 20),
    )(*outs)
    return (*outs[:5], outs[5].reshape(HD), outs[6].reshape(HD))


def solution(mesh):
    rows = P(("grp", "dev"), None)
    return jax.shard_map(
        shards,
        mesh=mesh,
        in_specs=(rows,) * 7 + (P(), P(), P("grp", None), P("grp", None)),
        out_specs=(rows,) * 5 + (P(), P()),
        check_vma=False,
    )
```

time: 71 us -> 51.4 us (0.72)
  local copies, waits for them, and re-layouts: 10.7 us -> 0 us
  Pallas kernels: 59.2 us -> 50.6 us
    unnamed x29 -> x0, local copies, waits for them, and re-layouts: 10.7 us -> none
    pallas_call x1 -> x2, Pallas kernels: 59.2 us -> 50.6 us  [the longest x1 48.8 us: shards(): pl.pallas_call(kernel, name='attention_backward', out_shape=shapes, in_sp...]
where the time goes in v2:
time: 51.4 us; the launch traced here: 51.3 us
  Pallas kernels  50.6 us (98%)
  between operations  0.64 us (1%)
    pallas_call x1, Pallas kernels, shards(): pl.pallas_call(kernel, name='attention_backward', out_shape=shapes, in_sp...  48.8 us
    pallas_call x1, Pallas kernels, shards(): pl.pallas_call(deliver, name='deliver', out_shape=shapes, in_specs=[somew...  1.85 us

profile of v2, /device:TPU:1, one launch (start us, length us, event | category | flops | bytes accessed | tf_op | source)
XLA Modules:
  0.0 51.3 jit_solution(10209281354934415491)
XLA Ops:
  0.6 48.8 %attention_backward.1 = (bf16[64,1024]{1,0:T(8,128)(2,1)}, bf16[64,128]{1,0:T(8,128)(2,1)}, bf16[64,128]{1,0:T(8,128)(2,1)}, f32[256,128]{1,0:T(8,128)}, f32[256...) custom-call(bf16[64,1024]{1,0:T(8,128)(2,1)} %qr_in.1, bf16[64,128]{1,0:T(8,128)(2,1)} %kr_in.1, ...), custom_call_target="tpu_custom_call" | custom-call | tf_op jit(solution)/shard_map/attention_backward/pallas_call | solution.py:489
  49.4 1.8 %deliver.1 = (bf16[64,1024]{1,0:T(8,128)(2,1)}, bf16[64,128]{1,0:T(8,128)(2,1)}, bf16[64,128]{1,0:T(8,128)(2,1)}, f32[256,128]{1,0:T(8,128)}, f32[256,128]{1,0:T...) custom-call(bf16[64,1024]{1,0:T(8,128)(2,1)} %get-tuple-element.21.refs_0_, bf16[64,128]{1,0:T(8,128)(2,1)} %get-tuple-element.22.refs_1_, ...), custom_call_target="tpu_custom_call" | custom-call | tf_op jit(solution)/shard_map/deliver/pallas_call | solution.py:547

commit v3 on v2

--- a/solution.py
+++ b/solution.py
@@ -20,8 +20,8 @@
 NT = (((1,), (1,)), ((), ()))
 NN = (((1,), (0,)), ((), ()))
 TN = (((0,), (0,)), ((), ()))
-S_Q, S_D, S_K, S_N, S_G, S_R, S_Z, S_X, S_Y, S_V, S_C = 0, 8, 12, 28, 32, 36, 52, 54, 58, 62, 70
-N_SEM = 71
+S_Q, S_D, S_K, S_N, S_G, S_R, S_Z, S_X, S_Y, S_V = 0, 8, 12, 28, 32, 36, 52, 54, 62, 66
+N_SEM = 74
 
 
 def dot(a, b, dims):
@@ -30,11 +30,11 @@
 
 def kernel(
     qr_in, kr_in, rv_in, ao_in, og_in, pk_in, pv_in, qg_in, kg_in, len_in, hold_in,
-    oq_out, ok_out, ov_out, opk_out, opv_out, oqg_out, okg_out,
-    oq_ref, ok_ref, ov_ref, opk_ref, opv_ref, oqg_ref, okg_ref,
+    oq_out, ok_out, ov_out, opk_out, opv_out, zr_out, gx_out,
+    oq_ref, ok_ref, ov_ref, opk_ref, opv_ref,
     qr_ref, kr_ref, rv_ref, ao_ref, og_ref, qg_ref, kg_ref, len_ref, hold_ref,
     qb, db, kb, kt, eg, dqt, rs, rss, rsr, qn, invr, dqs, dqsend, dqr,
-    se, sg, sb, acc, rr, zs, zr, gx, gy, gz, gc, gsrc, send, recv, load, store,
+    se, sg, sb, acc, rr, zs, gy, gz, gsrc, send, recv, load, store,
 ):
     grp = lax.axis_index("grp")
     dev = lax.axis_index("dev")
@@ -84,19 +84,19 @@
         )
 
     def z_copy(t):
-        return copy(zs.at[t], zr.at[t], S_Z + t, zk(4))
-
-    def gx_copy(k):
-        return copy(gsrc.at[0], gx.at[x], S_X + k, xk(k))
+        return copy(zs.at[t], zr_out.at[t], S_Z + t, zk(4))
+
+    def gx_to(k):
+        return at(x=(x + 4 - k // 2) % 4, core=(core + k) % 2)
+
+    def gz_copy(k):
+        return copy(gsrc.at[0], gz.at[z], S_V + k, zk(k))
 
     def gy_copy(k):
         return copy(gsrc.at[1], gy.at[y], S_Y + k, yk(k))
 
-    def gz_copy(k):
-        return copy(gsrc.at[2], gz.at[z], S_V + k, zk(k))
-
-    def gc_copy():
-        return copy(gsrc.at[3], gc.at[core], S_C, at(core=1 - core))
+    def gx_copy(k):
+        return copy(gsrc.at[2], gx_out.at[x * 2 + core], S_X + k, gx_to(k))
 
     loads = [
         pltpu.make_async_copy(src, dst, load.at[n])
@@ -116,14 +116,14 @@
         for n, (src, dst) in enumerate(
             (
                 (oq_ref, oq_out), (ok_ref, ok_out), (ov_ref, ov_out), (opk_ref, opk_out),
-                (opv_ref, opv_out), (oqg_ref, oqg_out), (okg_ref, okg_out),
+                (opv_ref, opv_out), (gsrc.at[2], gx_out.at[x * 2 + core]),
             )
         )
     ]
 
     barrier = pltpu.get_barrier_semaphore()
-    partners = [xk(k) for k in (1, 2, 3)] + [yk(k) for k in (1, 2, 3)]
-    partners += [zk(k) for k in range(1, 8)] + [at(core=1 - core)]
+    partners = [gx_to(k) for k in range(1, 8)] + [yk(k) for k in (1, 2, 3)]
+    partners += [zk(k) for k in range(1, 8)]
     for to in partners:
         pl.semaphore_signal(barrier, inc=1, device_id=to, device_id_type=MESH)
 
@@ -275,7 +275,7 @@
         kt[1, :, j * KEYS : (j + 1) * KEYS] = kb[4 + j, 0].T
 
     def rest(m, carry):
-        i = (m + 2) % 4
+        i = jnp.where(m == 2, 1, m + 2)
         dqt[i] += dot(kt[1], eg[1, 4:8, i].reshape(4 * KEYS, ROWS), NN)
         dqsend[i] = dqt[i].astype(bf16)
 
@@ -287,9 +287,7 @@
 
         return carry
 
-    lax.fori_loop(0, 4, rest, 0)
-    dqt[0] += dqs[...]
-    dqsend[0] = dqt[0].astype(bf16)
+    lax.fori_loop(0, 3, rest, 0)
     for k in (1, 3, 2):
         n_copy(k).wait_recv()
     for i in range(4):
@@ -319,6 +317,9 @@
         z_copy(t).start()
 
     def own_terms():
+        last = dot(kt[1], eg[1, 4:8, 0].reshape(4 * KEYS, ROWS), NN)
+        dqt[0] = dqt[0] + dqs[...] + last
+        dqsend[0] = dqt[0].astype(bf16)
         ov_ref[...] = dot(se[...], qn[0, 0], NN).astype(bf16)
         kng = dot(sg[...], qn[1, 0], NN)
         wide = kr_ref[...].astype(f32)
@@ -337,37 +338,29 @@
         query_gain = jnp.sum(jnp.where(one == two, square, 0.0), axis=0, keepdims=True) / gain
         both = jnp.concatenate([query_gain, key_gain, jnp.zeros((6, HD), f32)], axis=0)
         gsrc[0] = both
-        gx[x] = both
-        for k in (2, 1, 3):
-            gx_copy(k).start()
-
-    def gains_y():
-        for k in (1, 3, 2):
-            gx_copy(k).wait_recv()
-        both = gx[0] + gx[1] + gx[2] + gx[3]
-        gsrc[1] = both
-        gy[y] = both
-        for k in (2, 1, 3):
-            gy_copy(k).start()
-
-    def gains_z():
-        for k in (1, 3, 2):
-            gy_copy(k).wait_recv()
-        both = gy[0] + gy[1] + gy[2] + gy[3]
-        gsrc[2] = both
         gz[z] = both
         for k in (4, 3, 5, 2, 6, 1, 7):
             gz_copy(k).start()
 
-    def gains_core():
+    def gains_y():
         for k in range(1, 8):
             gz_copy(k).wait_recv()
         both = gz[0]
         for k in range(1, 8):
             both = both + gz[k]
-        gsrc[3] = both
-        gc[core] = both
-        gc_copy().start()
+        gsrc[1] = both
+        gy[y] = both
+        for k in (2, 1, 3):
+            gy_copy(k).start()
+
+    def gains_x():
+        for k in (1, 3, 2):
+            gy_copy(k).wait_recv()
+        both = gy[0] + gy[1] + gy[2] + gy[3]
+        gsrc[2] = both
+        stores[5].start()
+        for k in (4, 5, 2, 3, 6, 7, 1):
+            gx_copy(k).start()
 
     def terms(n, carry):
         plane = 1 - n // 8
@@ -375,21 +368,19 @@
         m = n % 4
         kk = jnp.where(m == 0, 2, jnp.where(m == 2, 3, jnp.where(m == 3, 0, 1)))
 
-        @pl.when(n == 4)
+        @pl.when(n == 2)
         def _():
             own_terms()
 
-        @pl.when(n == 8)
+        @pl.when(n == 12)
+        def _():
+            to_plane(0)
+
+        @pl.when(n == 14)
         def _():
             gains_y()
-
-        @pl.when(n == 12)
-        def _():
-            to_plane(0)
-
-        @pl.when(n == 13)
-        def _():
-            gains_z()
+            for k in (1, 3, 2):
+                r_copy(0, 0, k).start()
 
         j = plane * 4 + kk
         part = dot(eg[t, j, 0], qn[t, 0], NN)
@@ -397,9 +388,9 @@
             part = part + dot(eg[t, j, i], qn[t, i], NN)
         sb[plane, t, kk] = part.astype(bf16)
 
-        @pl.when(m < 3)
-        def _():
-            r_copy(plane, t, kk).start()
+        @pl.when((m < 3) & (n < 8))
+        def _():
+            r_copy(1, t, kk).start()
 
         @pl.when(m == 3)
         def _():
@@ -409,6 +400,8 @@
 
     lax.fori_loop(0, 16, terms, 0)
     to_plane(1)
+    for k in (1, 3, 2):
+        r_copy(0, 1, k).start()
 
     for k in (1, 3, 2):
         g_copy(k).wait_recv()
@@ -426,21 +419,15 @@
             oq_ref[:, h * HD : (h + 1) * HD] = found.astype(bf16)
     stores[0].start()
 
+    gains_x()
     opv_ref[...] = plane_sum(0, 0)
+    stores[4].start()
     opk_ref[...] = plane_sum(0, 1)
-    gains_core()
-    z_copy(0).wait_recv()
-    opv_ref[...] += zr[0].astype(f32)
-    stores[4].start()
-    z_copy(1).wait_recv()
-    opk_ref[...] += zr[1].astype(f32)
     stores[3].start()
-    gc_copy().wait_recv()
-    both = gc[0] + gc[1]
-    oqg_ref[...] = both[0:1, :]
-    okg_ref[...] = both[1:2, :]
-    stores[5].start()
-    stores[6].start()
+    for k in range(1, 8):
+        gx_copy(k).wait_recv()
+    for t in range(2):
+        z_copy(t).wait_recv()
 
     for p in range(2):
         for j in range(1, 8):
@@ -448,7 +435,7 @@
         for k in (1, 2, 3):
             q_copy(k, p).wait_send()
     for k in (1, 2, 3):
-        for make in (d_copy, n_copy, g_copy, gx_copy, gy_copy):
+        for make in (d_copy, n_copy, g_copy, gy_copy):
             make(k).wait_send()
         for plane in range(2):
             for t in range(2):
@@ -457,20 +444,35 @@
         z_copy(t).wait_send()
     for k in range(1, 8):
         gz_copy(k).wait_send()
-    gc_copy().wait_send()
+        gx_copy(k).wait_send()
     for one in stores:
         one.wait()
 
 
 def deliver(*refs):
-    into, out = refs[21], refs[22]
-    first = [pltpu.make_async_copy(refs[i], refs[14 + i], into.at[i]) for i in range(7)]
-    then = [pltpu.make_async_copy(refs[14 + i], refs[7 + i], out.at[i]) for i in range(7)]
+    ins, outs, held, ends, into, out = (
+        refs[:7], refs[7:14], refs[14:21], refs[21:23], refs[23], refs[24],
+    )
+    first = [pltpu.make_async_copy(ins[i], held[i], into.at[i]) for i in range(7)]
+    then = [
+        pltpu.make_async_copy(src, outs[i], out.at[i])
+        for i, src in enumerate((*held[:5], *ends))
+    ]
     for one in first:
         one.start()
-    for one, two in zip(first, then, strict=True):
+    for one in first:
         one.wait()
-        two.start()
+    held[3][...] += held[5][1].astype(f32)
+    then[3].start()
+    held[4][...] += held[5][0].astype(f32)
+    for i in (4, 0, 1, 2):
+        then[i].start()
+    both = held[6][0]
+    for k in range(1, 8):
+        both = both + held[6][k]
+    for i in range(2):
+        ends[i][...] = both[i : i + 1, :]
+        then[5 + i].start()
     for two in then:
         two.wait()
 
@@ -482,14 +484,17 @@
         jax.ShapeDtypeStruct((CAP, HD), bf16),
         jax.ShapeDtypeStruct((KEYS, HD), f32),
         jax.ShapeDtypeStruct((KEYS, HD), f32),
-        jax.ShapeDtypeStruct((1, HD), f32),
-        jax.ShapeDtypeStruct((1, HD), f32),
+    )
+    gains = (jax.ShapeDtypeStruct((1, HD), f32),) * 2
+    arrived = (
+        jax.ShapeDtypeStruct((2, KEYS, HD), bf16),
+        jax.ShapeDtypeStruct((8, 8, HD), f32),
     )
     somewhere = pl.BlockSpec(memory_space=pl.ANY)
     outs = pl.pallas_call(
         kernel,
         name="attention_backward",
-        out_shape=shapes,
+        out_shape=(*shapes, *arrived),
         in_specs=[somewhere] * 11,
         out_specs=(somewhere,) * 7,
         scratch_shapes=[
@@ -498,8 +503,6 @@
             pltpu.VMEM((CAP, HD), bf16),
             pltpu.VMEM((KEYS, HD), f32),
             pltpu.VMEM((KEYS, HD), f32),
-            pltpu.VMEM((1, HD), f32),
-            pltpu.VMEM((1, HD), f32),
             pltpu.VMEM((CAP, HEADS * HD), bf16),
             pltpu.VMEM((CAP, HD), bf16),
             pltpu.VMEM((CAP, HD), bf16),
@@ -529,16 +532,13 @@
             pltpu.VMEM((2, 2, KEYS, HD), f32),
             pltpu.VMEM((2, 2, 4, KEYS, HD), bf16),
             pltpu.VMEM((2, KEYS, HD), bf16),
-            pltpu.VMEM((2, KEYS, HD), bf16),
-            pltpu.VMEM((4, 8, HD), f32),
             pltpu.VMEM((4, 8, HD), f32),
             pltpu.VMEM((8, 8, HD), f32),
-            pltpu.VMEM((2, 8, HD), f32),
-            pltpu.VMEM((4, 8, HD), f32),
+            pltpu.VMEM((3, 8, HD), f32),
             pltpu.SemaphoreType.DMA((N_SEM,)),
             pltpu.SemaphoreType.DMA((N_SEM,)),
             pltpu.SemaphoreType.DMA((11,)),
-            pltpu.SemaphoreType.DMA((7,)),
+            pltpu.SemaphoreType.DMA((6,)),
         ],
         compiler_params=pltpu.CompilerParams(
             collective_id=0, has_side_effects=True, vmem_limit_bytes=60 << 20
@@ -547,10 +547,10 @@
     outs = pl.pallas_call(
         deliver,
         name="deliver",
-        out_shape=shapes,
+        out_shape=(*shapes, *gains),
         in_specs=[somewhere] * 7,
         out_specs=(somewhere,) * 7,
-        scratch_shapes=[pltpu.VMEM(shape.shape, shape.dtype) for shape in shapes]
+        scratch_shapes=[pltpu.VMEM(shape.shape, shape.dtype) for shape in (*shapes, *arrived, *gains)]
         + [pltpu.SemaphoreType.DMA((7,))] * 2,
         compiler_params=pltpu.CompilerParams(vmem_limit_bytes=60 << 20),
     )(*outs)

time: 51.4 us -> 49.3 us (0.959)
  Pallas kernels: 50.6 us -> 48.6 us
    pallas_call x2, Pallas kernels: 50.6 us -> 48.6 us  [the longest x1 46.6 us: shards(): pl.pallas_call(kernel, name='attention_backward', out_shape=(*shapes, *ar...]
where the time goes in v3:
time: 49.3 us; the launch traced here: 49.2 us
  Pallas kernels  48.6 us (99%)
  between operations  0.64 us (1%)
    pallas_call x1, Pallas kernels, shards(): pl.pallas_call(kernel, name='attention_backward', out_shape=(*shapes, *ar...  46.6 us
    pallas_call x1, Pallas kernels, shards(): pl.pallas_call(deliver, name='deliver', out_shape=(*shapes, *gains), in_s...  2.02 us

profile of v3, /device:TPU:1, one launch (start us, length us, event | category | flops | bytes accessed | tf_op | source)
XLA Modules:
  0.0 49.2 jit_solution(10044181247715653965)
XLA Ops:
  0.6 46.6 %attention_backward.1 = (bf16[64,1024]{1,0:T(8,128)(2,1)}, bf16[64,128]{1,0:T(8,128)(2,1)}, bf16[64,128]{1,0:T(8,128)(2,1)}, f32[256,128]{1,0:T(8,128)}, f32[256...) custom-call(bf16[64,1024]{1,0:T(8,128)(2,1)} %qr_in.1, bf16[64,128]{1,0:T(8,128)(2,1)} %kr_in.1, ...), custom_call_target="tpu_custom_call" | custom-call | tf_op jit(solution)/shard_map/attention_backward/pallas_call | solution.py:494
  47.2 2.0 %deliver.1 = (bf16[64,1024]{1,0:T(8,128)(2,1)}, bf16[64,128]{1,0:T(8,128)(2,1)}, bf16[64,128]{1,0:T(8,128)(2,1)}, f32[256,128]{1,0:T(8,128)}, f32[256,128]{1,0:T...) custom-call(bf16[64,1024]{1,0:T(8,128)(2,1)} %get-tuple-element.21.refs_0_, bf16[64,128]{1,0:T(8,128)(2,1)} %get-tuple-element.22.refs_1_, ...), custom_call_target="tpu_custom_call" | custom-call | tf_op jit(solution)/shard_map/deliver/pallas_call | solution.py:547

commit v4 on v3

--- a/solution.py
+++ b/solution.py
@@ -376,7 +376,7 @@
         def _():
             to_plane(0)
 
-        @pl.when(n == 14)
+        @pl.when(n == 12)
         def _():
             gains_y()
             for k in (1, 3, 2):

time: 49.3 us -> 49 us (level)
  no operation moved by 1% of the time
where the time goes in v4:
time: 49 us; the launch traced here: 48.9 us
  Pallas kernels  48.3 us (99%)
  between operations  0.64 us (1%)
    pallas_call x1, Pallas kernels, shards(): pl.pallas_call(kernel, name='attention_backward', out_shape=(*shapes, *ar...  46.3 us
    pallas_call x1, Pallas kernels, shards(): pl.pallas_call(deliver, name='deliver', out_shape=(*shapes, *gains), in_s...  2.02 us

profile of v4, /device:TPU:1, one launch (start us, length us, event | category | flops | bytes accessed | tf_op | source)
XLA Modules:
  0.0 48.9 jit_solution(17915863295148619948)
XLA Ops:
  0.6 46.3 %attention_backward.1 = (bf16[64,1024]{1,0:T(8,128)(2,1)}, bf16[64,128]{1,0:T(8,128)(2,1)}, bf16[64,128]{1,0:T(8,128)(2,1)}, f32[256,128]{1,0:T(8,128)}, f32[256...) custom-call(bf16[64,1024]{1,0:T(8,128)(2,1)} %qr_in.1, bf16[64,128]{1,0:T(8,128)(2,1)} %kr_in.1, ...), custom_call_target="tpu_custom_call" | custom-call | tf_op jit(solution)/shard_map/attention_backward/pallas_call | solution.py:494
  46.9 2.0 %deliver.1 = (bf16[64,1024]{1,0:T(8,128)(2,1)}, bf16[64,128]{1,0:T(8,128)(2,1)}, bf16[64,128]{1,0:T(8,128)(2,1)}, f32[256,128]{1,0:T(8,128)}, f32[256,128]{1,0:T...) custom-call(bf16[64,1024]{1,0:T(8,128)(2,1)} %get-tuple-element.21.refs_0_, bf16[64,128]{1,0:T(8,128)(2,1)} %get-tuple-element.22.refs_1_, ...), custom_call_target="tpu_custom_call" | custom-call | tf_op jit(solution)/shard_map/deliver/pallas_call | solution.py:547

commit v5 on v4

--- a/solution.py
+++ b/solution.py
@@ -199,6 +199,12 @@
         g = e * (dot(values, qb[i, 1], NT) - db[i])
         return e.astype(bf16), g.astype(bf16)
 
+    def pass_on(p):
+        k_copy(4, p).wait_recv()
+        for j in (5, 7, 6):
+            k_copy(j, p).start()
+
+    pass_on(0)
     q_copy(3, 0).wait_recv()
     q_copy(2, 0).start()
     q_copy(1, 1).wait_recv()
@@ -210,19 +216,13 @@
     for j in (1, 3, 2):
         k_copy(j, 1).wait_recv()
 
-    def pass_on(p):
-        k_copy(4, p).wait_recv()
-        for j in (5, 7, 6):
-            k_copy(j, p).start()
-
-    pass_on(0)
+    pass_on(1)
 
     def near(m, carry):
         i = jnp.where(m == 2, 3, jnp.where(m == 3, 2, m))
 
         @pl.when(m == 1)
         def _():
-            pass_on(1)
             q_copy(1, 0).wait_recv()
             d_copy(1).wait_recv()
 
@@ -368,7 +368,7 @@
         m = n % 4
         kk = jnp.where(m == 0, 2, jnp.where(m == 2, 3, jnp.where(m == 3, 0, 1)))
 
-        @pl.when(n == 2)
+        @pl.when(n == 1)
         def _():
             own_terms()
 
@@ -402,6 +402,8 @@
     to_plane(1)
     for k in (1, 3, 2):
         r_copy(0, 1, k).start()
+
+    gains_x()
 
     for k in (1, 3, 2):
         g_copy(k).wait_recv()
@@ -419,7 +421,6 @@
             oq_ref[:, h * HD : (h + 1) * HD] = found.astype(bf16)
     stores[0].start()
 
-    gains_x()
     opv_ref[...] = plane_sum(0, 0)
     stores[4].start()
     opk_ref[...] = plane_sum(0, 1)

time: 49 us -> 49.1 us (level)
  no operation moved by 1% of the time
where the time goes in v5:
time: 49.1 us; the launch traced here: 49 us
  Pallas kernels  48.4 us (99%)
  between operations  0.64 us (1%)
    pallas_call x1, Pallas kernels, shards(): pl.pallas_call(kernel, name='attention_backward', out_shape=(*shapes, *ar...  46.4 us
    pallas_call x1, Pallas kernels, shards(): pl.pallas_call(deliver, name='deliver', out_shape=(*shapes, *gains), in_s...  2.02 us

profile of v5, /device:TPU:1, one launch (start us, length us, event | category | flops | bytes accessed | tf_op | source)
XLA Modules:
  0.0 49.0 jit_solution(11783209502427458047)
XLA Ops:
  0.6 46.4 %attention_backward.1 = (bf16[64,1024]{1,0:T(8,128)(2,1)}, bf16[64,128]{1,0:T(8,128)(2,1)}, bf16[64,128]{1,0:T(8,128)(2,1)}, f32[256,128]{1,0:T(8,128)}, f32[256...) custom-call(bf16[64,1024]{1,0:T(8,128)(2,1)} %qr_in.1, bf16[64,128]{1,0:T(8,128)(2,1)} %kr_in.1, ...), custom_call_target="tpu_custom_call" | custom-call | tf_op jit(solution)/shard_map/attention_backward/pallas_call | solution.py:495
  47.0 2.0 %deliver.1 = (bf16[64,1024]{1,0:T(8,128)(2,1)}, bf16[64,128]{1,0:T(8,128)(2,1)}, bf16[64,128]{1,0:T(8,128)(2,1)}, f32[256,128]{1,0:T(8,128)}, f32[256,128]{1,0:T...) custom-call(bf16[64,1024]{1,0:T(8,128)(2,1)} %get-tuple-element.21.refs_0_, bf16[64,128]{1,0:T(8,128)(2,1)} %get-tuple-element.22.refs_1_, ...), custom_call_target="tpu_custom_call" | custom-call | tf_op jit(solution)/shard_map/deliver/pallas_call | solution.py:548
